TPU v7x, 32 devices: a whole 2x2x4 slice. The times are simulated.
32 devices in a mesh: rec: 4 (over y, core), tract: 8 (over z, x).
Axes of the slice: x: 2, y: 2, z: 4, core: 2. Of those that a mesh axis runs over, the one named last changes fastest.
Arguments:
- rep_weights: float32 [80, 131072], P(None, ('rec', 'tract')), may hold values from 0.5 to 2
- covariate_codes: int32 [5, 131072], P(None, ('rec', 'tract')), may hold values from 0 to 15
- tract_of: int32 [131072, 1], P(('rec', 'tract')), may hold values from 0 to 7; in each aligned block of 4096 rows (0 to 4095, 4096 to 8191, ...) at most 1536 rows name the same one
- log_income: bfloat16 [131072], P(('rec', 'tract')), may hold values from -5 to 5
- controls: float32 [64], replicated, may hold values from 7782 to 10240
- threshold_grid: int32 [2048], replicated, may hold values from 0 to 4095
Outputs:
- calibrated: float32 [80, 131072], P(None, ('rec', 'tract'))
- income_tables: float32 [8, 80, 2048], P('tract', None, 'rec')
Inputs may be any that keep to these rules, and one draw needn't show every extreme that they name: `tract_of`: among the 4096 persons of one device at most 1536 share a tract; in some aligned blocks of 4096 persons one tract has exactly 1536.
All inputs are finite; a program needn't handle non-finite values.
Results may differ from a plain program's by a relative error of at most 0.0003.
Values may be sent and summed in bfloat16 or wider, within the bound.
A program may use at most 128 MiB of HBM per device.

v0:
```python
import math

import jax
import jax.numpy as jnp
from jax import lax
from jax.sharding import PartitionSpec as P

smooth_width = 3.0 / 8192.0
grid_middle = 2048.0
grid_step = 3.0 / 2048.0
base_levels = 16
first_kept = 4


def design(covariate_codes):
    level_codes = jnp.arange(base_levels, dtype=jnp.int32)
    kept_levels = jnp.arange(first_kept, base_levels, dtype=jnp.int32)
    groups = [covariate_codes[0][None, :] == level_codes[:, None]]
    for variable in range(1, covariate_codes.shape[0]):
        groups.append(covariate_codes[variable][None, :] == kept_levels[:, None])
    return jnp.concatenate(groups, axis=0).astype(jnp.float32)


def solve_controls(gram_sums, totals, controls):
    factor = jnp.linalg.cholesky(gram_sums)
    gap = (controls[None, :] - totals)[:, :, None]
    middle = lax.linalg.triangular_solve(factor, gap, left_side=True, lower=True)
    result = lax.linalg.triangular_solve(
        factor, middle, left_side=True, lower=True, transpose_a=True
    )
    return result[:, :, 0]


def shards(rep_weights, covariate_codes, tract_of, log_income, controls, threshold_grid):
    rep_count, row_count = rep_weights.shape
    ctrl_count = controls.shape[0]
    tract_count = lax.axis_size("tract")
    rec_count = lax.axis_size("rec")
    design_rows = design(covariate_codes)
    block_rows = math.gcd(row_count, 256)

    def gram_step(position, running):
        weight_block = lax.dynamic_slice_in_dim(rep_weights, position * block_rows, block_rows, 1)
        design_block = lax.dynamic_slice_in_dim(design_rows, position * block_rows, block_rows, 1)
        spread = (weight_block[:, None, :] * design_block[None, :, :]).reshape(
            rep_count * ctrl_count, block_rows
        )
        product = jnp.einsum("an,cn->ac", spread, design_block, precision=lax.Precision.HIGHEST)
        return running + product.reshape(rep_count, ctrl_count, ctrl_count)

    gram_sums = lax.fori_loop(
        0,
        row_count // block_rows,
        gram_step,
        jnp.zeros((rep_count, ctrl_count, ctrl_count), jnp.float32),
    )
    totals = jnp.einsum("rn,cn->rc", rep_weights, design_rows, precision=lax.Precision.HIGHEST)
    gram_sums, totals = lax.psum((gram_sums, totals), ("rec", "tract"))
    multipliers = solve_controls(gram_sums, totals, controls)
    factors = 1.0 + jnp.dot(multipliers, design_rows, precision=lax.Precision.HIGHEST)
    calibrated = rep_weights * factors
    sent_weights = calibrated.astype(jnp.bfloat16)
    centers = (threshold_grid.astype(jnp.float32) - grid_middle) * grid_step
    tract_ids = tract_of[:, 0]
    per_tract = float(row_count * rec_count)
    capacity = 3 * row_count // tract_count
    belongs = (tract_ids[:, None] == jnp.arange(tract_count, dtype=jnp.int32)[None, :]).astype(
        jnp.int32
    )
    earlier = jnp.cumsum(belongs, axis=0) - belongs
    slot_index = jnp.sum(earlier * belongs, axis=1)
    target = tract_ids * capacity + slot_index
    source = jnp.full((tract_count * capacity,), row_count, jnp.int32)
    source = source.at[target].set(jnp.arange(row_count, dtype=jnp.int32))
    payload = jnp.concatenate([sent_weights, log_income[None, :]], axis=0)
    payload = jnp.concatenate([payload, jnp.zeros((rep_count + 1, 1), jnp.bfloat16)], axis=1)
    buffer = jnp.take(payload, source.reshape(tract_count, capacity), axis=1)
    received = lax.all_to_all(buffer, "tract", split_axis=1, concat_axis=1, tiled=True)
    recv_weights = received[:rep_count]
    recv_income = received[rep_count].astype(jnp.float32)
    smoothed = jax.nn.sigmoid((centers[None, None, :] - recv_income[:, :, None]) / smooth_width)
    smoothed = smoothed.astype(jnp.bfloat16)
    term = lax.psum_scatter(
        jnp.einsum("rsm,smj->jr", recv_weights, smoothed, preferred_element_type=jnp.float32),
        "rec",
        scatter_dimension=0,
        tiled=True,
    )
    income_tables = (term.T / per_tract)[None]
    return (calibrated, income_tables)


def solution(mesh):
    placed = (
        P(None, ("rec", "tract")),
        P(None, ("rec", "tract")),
        P(("rec", "tract"), None),
        P(("rec", "tract")),
        P(),
        P(),
    )
    return jax.shard_map(
        shards,
        mesh=mesh,
        in_specs=placed,
        out_specs=(P(None, ("rec", "tract")), P("tract", None, "rec")),
        check_vma=False,
    )
```

profile of v0, /device:TPU:11, one launch (start us, length us, event | category | flops | bytes accessed | tf_op | source)
XLA Modules:
  0.0 994.6 jit_solution(17329571507120278312)
XLA Ops:
  9.0 13.0 %concatenate.9 = pred[64,4096]{1,0:T(32,128)(4,1)S(1)} concatenate(pred[16,4096]{1,0:T(8,128)(4,1)S(1)} %iota_compare_fusion, pred[12,4096]{1,0:T(8,128)(4,1)S(1)} %get-tuple-element.113, pred[12,4096]{1,0:T(8,128)(4,1)S(1)} %get-tuple-element.111, pred[12,4096]{1,0:T(8,128)(4,1)S(1)} %get-tuple-element.112, pred[12,4096]{1,0:T(8,128)(4,1)S(1)} %get-tuple-element.110), dimensions={0} | concatenate | bytes 524288 | tf_op jit(solution)/shard_map/concatenate | solution.py:21
  23.1 109.5 %while.14 = (s32[]{:T(128)}, f32[80,64,64]{2,1,0:T(8,128)S(1)}, f32[80,4096]{1,0:T(8,128)}, f32[64,4096]{1,0:T(8,128)}, s32[]{:T(128)}, /*index=5*/s32[]{:T(128)}, s32[]{:T(128)}, s32[]{:T(128)}) while((s32[]{:T(128)}, f32[80,64,64]{2,1,0:T(8,128)S(1)}, f32[80,4096]{1,0:T(8,128)}, f32[64,4096]{1,0:T(8,128)}, s32[]{:T(128)}, ...), condition=%wide.region_1.0_spmd.clone, body=%wide.region_0.0_spmd.clone.sunk | while | flops 1008599040 | bytes 3063957 | solution.py:51
  24.9 5.1 select_add_fusion.2
  31.7 5.1 select_add_fusion.2
  38.6 5.1 select_add_fusion.2
  45.4 5.1 select_add_fusion.2
  52.3 5.1 select_add_fusion.2
  59.1 5.1 select_add_fusion.2
  66.0 5.1 select_add_fusion.2
  72.8 5.1 select_add_fusion.2
  79.7 5.1 select_add_fusion.2
  86.5 5.1 select_add_fusion.2
  93.3 5.1 select_add_fusion.2
  100.2 5.1 select_add_fusion.2
  107.0 5.1 select_add_fusion.2
  113.9 5.1 select_add_fusion.2
  120.7 5.1 select_add_fusion.2
  127.6 5.1 select_add_fusion.2
  140.0 15.5 %scatter_custom_fusion = s32[12288]{0:T(1024)S(1)} fusion(s32[4096]{0:T(1024)S(1)} %bitcast.84, s32[4096]{0:T(1024)S(1)} %iota.52, s32[]{:T(128)} %constant.113.clone.1), kind=kCustom, calls=%fused_computation.50 | custom fusion | bytes 49156 | tf_op jit(solution)/shard_map/scatter | solution.py:74
  155.6 40.1 %psum.15 = f32[80,64]{0,1:T(8,128)S(1)} all-reduce(f32[80,64]{0,1:T(8,128)S(1)} %convolution_bitcast_fusion), channel_id=1, replica_groups=mesh['rec'=4,'tract'=8] {'rec','tract'}, use_global_device_ids=true, to_apply=%region_5.6 | all-reduce | flops 5120 | bytes 40960 | tf_op jit(solution)/shard_map/psum | solution.py:58
  195.9 74.6 %all-reduce.3.cloned.1.call-done = f32[80,64,64]{1,2,0:T(8,128)} async-done(((f32[80,64,64]{1,2,0:T(8,128)}), f32[80,64,64]{1,2,0:T(8,128)}) %all-reduce.3.cloned.1.call-update) | async-done | bytes 1310736 | tf_op jit(solution)/shard_map/psum | solution.py:58
  270.5 3.4 copy.21
  273.9 3.8 fusion.9
  277.7 470.7 %custom-call.9 = f32[80,64,64]{2,1,0:T(8,128)} custom-call(f32[80,64,64]{2,1,0:T(8,128)} %fusion.9), custom_call_target="Cholesky" | custom-call | tf_op jit(solution)/shard_map/jit(cholesky)/cholesky | solution.py:25
  753.6 67.2 %custom-call.10 = f32[80,1,64,64]{0,2,3,1:T(8,128)S(1)} custom-call(f32[80,1,64,64]{0,3,2,1:T(8,128)} %select_bitcast_fusion.1), custom_call_target="InvertDiagBlocksLowerTriangular" | custom-call | tf_op jit(solution)/shard_map/triangular_solve | solution.py:28
  822.2 3.6 copy.33
  825.7 4.2 fusion.23
  832.7 43.3 %gather_fusion = bf16[12288,81]{1,0:T(8,128)(2,1)} fusion(bf16[81,4097]{0,1:T(8,128)(2,1)S(1)} %concatenate.11.clone, s32[12288]{0:T(1024)S(1)} %broadcast_clamp_fusion), kind=kCustom, calls=%fused_computation | custom fusion | bytes 4030464 | tf_op jit(solution)/shard_map/jit(_take)/gather | solution.py:77
  881.0 4.5 all-to-all-start
  885.5 47.1 %all-to-all-done = bf16[81,8,1536]{2,0,1:T(8,128)(2,1)S(1)} async-done(((bf16[81,8,1536]{2,0,1:T(8,128)(2,1)}), bf16[81,8,1536]{2,0,1:T(8,128)(2,1)S(1)}, u32[]{:S(2)}, u32[]{:S(2)}) %all-to-all-start) | async-done | bytes 1990688 | tf_op jit(solution)/shard_map/all_to_all | solution.py:78
  932.6 29.7 %fusion.10 = f32[2048,80]{0,1:T(8,128)} fusion(f32[8,1536]{1,0:T(8,128)S(1)} %bitcast.82, f32[2048]{0:T(1024)S(1)} %add_multiply_fusion, bf16[81,8,1536]{2,0,1:T(8,128)(2,1)S(1)} %all-to-all-done), kind=kOutput, calls=%fused_computation.16 | convolution fusion | flops 4177526784 | bytes 2678784 | tf_op jit(solution)/shard_map/rsm,smj->jr/dot_general | solution.py:84
  962.3 23.9 %reduce-scatter.2.cloned.1.call-done = f32[512,80]{0,1:T(8,128)} async-done(((f32[2048,80]{0,1:T(8,128)}), f32[512,80]{0,1:T(8,128)}) %reduce-scatter.2.cloned.1.call-update) | async-done | bytes 163856 | tf_op jit(solution)/shard_map/reduce_scatter | solution.py:83
  (94 shorter events, 54.1 us)
Async XLA Ops:
  7.2 263.3 %all-reduce.3.cloned.1.call-start = ((), (), s32[]{:S(2)}) async-start(), calls=%async_computation.2 | async-start | bytes 5242880 | tf_op jit(solution)/shard_map/psum | solution.py:58
  134.8 1.3 copy-start.2
  134.8 2.1 copy-start.4
  134.8 60.9 %copy-start.5 = (bf16[4096]{0:T(1024)(128)(2,1)S(1)}, bf16[4096]{0:T(1024)(128)(2,1)}, u32[]{:S(2)}) copy-start(bf16[4096]{0:T(1024)(128)(2,1)} %param.11) | copy-start | bytes 24580
  134.8 61.0 %copy-start.7 = (f32[64]{0:T(128)S(1)}, f32[64]{0:T(128)}, u32[]{:S(2)}) copy-start(f32[64]{0:T(128)} %param.12) | copy-start | bytes 772
  270.5 3.4 copy-start
  820.8 1.4 copy-start.1
  825.7 4.2 copy-start.3
  881.0 4.5 copy-start.6
  881.0 51.6 %all-to-all-start = ((bf16[81,8,1536]{2,0,1:T(8,128)(2,1)}), bf16[81,8,1536]{2,0,1:T(8,128)(2,1)S(1)}, u32[]{:S(2)}, u32[]{:S(2)}) async-start(bf16[81,8,1536]{2,0,1:T(8,128)(2,1)} %select_bitcast_fusion), calls=%async_computation | async-start | bytes 4325376 | tf_op jit(solution)/shard_map/all_to_all | solution.py:78
  885.4 100.7 %reduce-scatter.2.cloned.1.call-start = ((), (), s32[]{:S(2)}) async-start(), calls=%async_computation.3 | async-start | bytes 819200 | tf_op jit(solution)/shard_map/reduce_scatter | solution.py:83
Sparse Core Ops, SparseCore 0:
  134.9 135.4 all-reduce.2
  962.4 23.7 reduce-scatter.1
where the time goes:
time: 998 us; the launch traced here: 995 us
  other arithmetic  552 us (55%)
  waiting for transfers between devices  146 us (15%)
  local copies, waits for them, and re-layouts  120 us (12%)
  matrix products  118 us (12%)
  blocking collectives  40.1 us (4%)
  between operations  14.4 us (1%)
    another operation x4, other arithmetic, solve_controls(): factor = jnp.linalg.cholesky(gram_sums)  471 us
    dot_general x16, matrix products, gram_step(): jnp.einsum('an,cn->ac', spread, design_block, precision=lax.Precision.HIG...  81.2 us
    psum x1, waiting for transfers between devices, shards(): gram_sums, totals = lax.psum((gram_sums, totals), ('rec', 'tract'))  74.6 us
    another operation x3, other arithmetic, solve_controls(): lax.linalg.triangular_solve(factor, middle, left_side=True, lower=True, t...  69 us
    all_to_all x1, waiting for transfers between devices, shards(): lax.all_to_all(buffer, 'tract', split_axis=1, concat_axis=1, tiled=True)  47.1 us
    gather x2, local copies, waits for them, and re-layouts, shards(): buffer = jnp.take(payload, source.reshape(tract_count, capacity), axis=1)  46.6 us
    psum x1, blocking collectives, shards(): gram_sums, totals = lax.psum((gram_sums, totals), ('rec', 'tract'))  40.1 us
    dot_general x1, matrix products, shards(): jnp.einsum('rsm,smj->jr', recv_weights, smoothed, preferred_element_type=...  29.7 us
  transfers between devices with their start and end apart: 3, of which 3 were waited for; matrix products, arithmetic and copies ran while one was open for 2% of the time, Pallas kernels for 0%

commit v1 on v0

v1 whole, which is shorter than its diff:
```python
import functools

import jax
import jax.numpy as jnp
from jax import lax
from jax.experimental import pallas as pl
from jax.experimental.pallas import tpu as pltpu
from jax.sharding import PartitionSpec as P

smooth_width = 3.0 / 8192.0
grid_middle = 2048.0
grid_step = 3.0 / 2048.0
base_levels = 16
first_kept = 4
vmem_bytes = 48 * 1024 * 1024
bf16 = jnp.bfloat16
f32 = jnp.float32


def pair_layout(variables):
    offsets, row = {}, 0
    for u in range(variables):
        first = 0 if u == 0 else first_kept
        for v in range(u + 1, variables):
            offsets[u, v] = row
            row += (base_levels - first) * base_levels
    singles = row
    row += variables * base_levels
    return offsets, singles, row


def split3(value, axis):
    high = value.astype(bf16)
    rest = value - high.astype(f32)
    middle = rest.astype(bf16)
    low = (rest - middle.astype(f32)).astype(bf16)
    return jnp.concatenate([high, middle, low], axis=axis)


def one_hot(key, rows):
    width = key.shape[1]
    row = lax.broadcasted_iota(jnp.int32, (rows, width), 0)
    return jnp.where(row == key, 1.0, 0.0).astype(bf16)


def gram_kernel(w_ref, codes_ref, out_ref, pairs, total):
    step = pl.program_id(0)
    variables, _ = codes_ref.shape
    reps = w_ref.shape[0]
    offsets, singles, rows = pair_layout(variables)

    @pl.when(step == 0)
    def _():
        total[...] = jnp.zeros_like(total)

    pieces = split3(w_ref[...], 0)
    for (u, v), row in offsets.items():
        first = 0 if u == 0 else first_kept
        key = (codes_ref[u : u + 1, :] - first) * base_levels + codes_ref[v : v + 1, :]
        count = (base_levels - first) * base_levels
        pairs[row : row + count, :] = one_hot(key, count)
    for v in range(variables):
        row = singles + v * base_levels
        pairs[row : row + base_levels, :] = one_hot(codes_ref[v : v + 1, :], base_levels)
    total[...] += lax.dot_general(
        pairs[...], pieces, (((1,), (1,)), ((), ())), preferred_element_type=f32
    )

    @pl.when(step == pl.num_programs(0) - 1)
    def _():
        out_ref[...] = (
            total[:, :reps] + total[:, reps : 2 * reps] + total[:, 2 * reps : 3 * reps]
        )


def gram(rep_weights, covariate_codes):
    reps, people = rep_weights.shape
    variables = covariate_codes.shape[0]
    rows = pair_layout(variables)[2]
    block = 1024
    return pl.pallas_call(
        gram_kernel,
        grid=(people // block,),
        in_specs=[
            pl.BlockSpec((reps, block), lambda i: (0, i)),
            pl.BlockSpec((variables, block), lambda i: (0, i)),
        ],
        out_specs=pl.BlockSpec((rows, reps), lambda i: (0, 0)),
        out_shape=jax.ShapeDtypeStruct((rows, reps), f32),
        scratch_shapes=[pltpu.VMEM((rows, block), bf16), pltpu.VMEM((rows, 3 * reps), f32)],
        compiler_params=pltpu.CompilerParams(vmem_limit_bytes=vmem_bytes),
        cost_estimate=pl.CostEstimate(
            flops=6 * rows * reps * people, bytes_accessed=4 * reps * people, transcendentals=0
        ),
    )(rep_weights, covariate_codes)


def solve_kernel(variables, sums_ref, controls_ref, out_ref, mat, rhs, coef, sol):
    size, _, reps = mat.shape
    offsets, singles, _ = pair_layout(variables)
    kept = base_levels - first_kept
    starts = [0] + [base_levels + kept * (v - 1) for v in range(1, variables)]
    firsts = [0] + [first_kept] * (variables - 1)
    mat[...] = jnp.zeros_like(mat)
    for v in range(variables):
        first, count = firsts[v], base_levels - firsts[v]
        single = sums_ref[singles + v * base_levels + first : singles + (v + 1) * base_levels, :]
        rhs[starts[v] : starts[v] + count, :] = (
            controls_ref[starts[v] : starts[v] + count, :] - single
        )
        for c in range(count):
            mat[starts[v] + c, starts[v] + c : starts[v] + c + 1, :] = single[c : c + 1, :]
    for (u, v), row in offsets.items():
        for c in range(base_levels - firsts[u]):
            at = row + c * base_levels + first_kept
            mat[starts[u] + c, starts[v] : starts[v] + kept, :] = sums_ref[at : at + kept, :]

    for block in range(size // 8):
        low = block * 8

        def eliminate(inner, carry, low=low, block=block):
            k = low + inner
            row = mat[k, low:, :]
            pivot = mat[k, pl.ds(k, 1), :]
            place = lax.broadcasted_iota(jnp.int32, row.shape, 0) + low
            factor = jnp.where(place > k, row * (1.0 / pivot), 0.0)
            coef[low:, :] = factor
            rhs[low:, :] = rhs[low:, :] - factor * rhs[pl.ds(k, 1), :]
            for other in range(block, size // 8):
                part = row[other * 8 - low :, :]
                for i in range(other * 8, other * 8 + 8):
                    mat[i, other * 8 :, :] = mat[i, other * 8 :, :] - coef[i : i + 1, :] * part
            return carry

        lax.fori_loop(0, 8, eliminate, 0)

    sol[...] = jnp.zeros_like(sol)
    for block in reversed(range(size // 8)):
        low = block * 8

        def substitute(inner, carry, low=low):
            k = low + 7 - inner
            known = jnp.sum(mat[k, low:, :] * sol[low:, :], axis=0, keepdims=True)
            sol[pl.ds(k, 1), :] = (rhs[pl.ds(k, 1), :] - known) / mat[k, pl.ds(k, 1), :]
            return carry

        lax.fori_loop(0, 8, substitute, 0)

    out_ref[...] = jnp.zeros_like(out_ref)
    for v in range(variables):
        count = base_levels - firsts[v]
        at = v * base_levels + firsts[v]
        out_ref[at : at + count, :] = sol[starts[v] : starts[v] + count, :]


def solve(sums, controls, variables):
    reps = sums.shape[1]
    size = controls.shape[0]
    return pl.pallas_call(
        functools.partial(solve_kernel, variables),
        in_specs=[pl.BlockSpec(memory_space=pltpu.VMEM)] * 2,
        out_specs=pl.BlockSpec(memory_space=pltpu.VMEM),
        out_shape=jax.ShapeDtypeStruct((variables * base_levels, reps), f32),
        scratch_shapes=[
            pltpu.VMEM((size, size, reps), f32),
            pltpu.VMEM((size, reps), f32),
            pltpu.VMEM((size, reps), f32),
            pltpu.VMEM((size, reps), f32),
        ],
        compiler_params=pltpu.CompilerParams(vmem_limit_bytes=vmem_bytes),
    )(sums, jnp.broadcast_to(controls[:, None], (size, reps)))


def calibrate_kernel(x_ref, w_ref, codes_ref, cal_ref, sent_ref):
    variables = codes_ref.shape[0]
    design = jnp.concatenate(
        [one_hot(codes_ref[v : v + 1, :], base_levels) for v in range(variables)], axis=0
    )
    pieces = split3(x_ref[...], 0)
    adjustment = lax.dot_general(
        pieces,
        jnp.concatenate([design] * 3, axis=0),
        (((0,), (0,)), ((), ())),
        preferred_element_type=f32,
    )
    calibrated = w_ref[...] * (1.0 + adjustment)
    cal_ref[...] = calibrated
    sent_ref[...] = calibrated.astype(bf16)


def calibrate(x, rep_weights, covariate_codes):
    reps, people = rep_weights.shape
    variables = covariate_codes.shape[0]
    block = 1024
    return pl.pallas_call(
        calibrate_kernel,
        grid=(people // block,),
        in_specs=[
            pl.BlockSpec(x.shape, lambda i: (0, 0)),
            pl.BlockSpec((reps, block), lambda i: (0, i)),
            pl.BlockSpec((variables, block), lambda i: (0, i)),
        ],
        out_specs=[pl.BlockSpec((reps, block), lambda i: (0, i))] * 2,
        out_shape=[
            jax.ShapeDtypeStruct((reps, people), f32),
            jax.ShapeDtypeStruct((reps, people), bf16),
        ],
        compiler_params=pltpu.CompilerParams(vmem_limit_bytes=vmem_bytes),
    )(x, rep_weights, covariate_codes)


def table_kernel(tracts, sent_ref, about_ref, grid_ref, out_ref, masked):
    step = pl.program_id(0) * pl.num_programs(1) + pl.program_id(1)
    reps = sent_ref.shape[1]
    sent = sent_ref[0]
    income = about_ref[0, 0:1, :]
    tract = about_ref[0, 1:2, :]
    for k in range(tracts):
        inside = jnp.where(tract == float(k), 1.0, 0.0).astype(bf16)
        masked[k * reps : (k + 1) * reps, :] = sent * inside
    centers = (grid_ref[...].astype(f32) - grid_middle) * grid_step
    half = (centers - income) * (0.5 / smooth_width)
    smoothed = (0.5 + 0.5 * jnp.tanh(half)).astype(bf16)
    product = lax.dot_general(
        masked[...], smoothed, (((1,), (1,)), ((), ())), preferred_element_type=f32
    )

    @pl.when(step == 0)
    def _():
        out_ref[...] = product

    @pl.when(step > 0)
    def _():
        out_ref[...] += product


def partial_tables(sent, about, grid_column, tracts):
    sources, reps, people = sent.shape
    thresholds = grid_column.shape[0]
    block = 1024
    return pl.pallas_call(
        functools.partial(table_kernel, tracts),
        grid=(sources, people // block),
        in_specs=[
            pl.BlockSpec((1, reps, block), lambda s, i: (s, 0, i)),
            pl.BlockSpec((1, 2, block), lambda s, i: (s, 0, i)),
            pl.BlockSpec((thresholds, 1), lambda s, i: (0, 0)),
        ],
        out_specs=pl.BlockSpec((tracts * reps, thresholds), lambda s, i: (0, 0)),
        out_shape=jax.ShapeDtypeStruct((tracts * reps, thresholds), f32),
        scratch_shapes=[pltpu.VMEM((tracts * reps, block), bf16)],
        compiler_params=pltpu.CompilerParams(vmem_limit_bytes=vmem_bytes),
    )(sent, about, grid_column)


def shards(rep_weights, covariate_codes, tract_of, log_income, controls, threshold_grid):
    reps, people = rep_weights.shape
    variables = covariate_codes.shape[0]
    tracts = lax.axis_size("tract")
    recs = lax.axis_size("rec")
    share = threshold_grid.shape[0] // recs
    grid_column = lax.dynamic_slice_in_dim(
        threshold_grid, lax.axis_index("rec") * share, share, 0
    )[:, None]
    about = jnp.stack([log_income.astype(f32), tract_of[:, 0].astype(f32)])
    about = lax.all_gather(about, "rec")
    sums = lax.psum(gram(rep_weights, covariate_codes), ("rec", "tract"))
    x = solve(sums, controls, variables)
    calibrated, sent = calibrate(x, rep_weights, covariate_codes)
    sent = lax.all_gather(sent, "rec")
    tables = partial_tables(sent, about, grid_column, tracts)
    tables = lax.psum_scatter(tables, "tract", scatter_dimension=0, tiled=True)
    return calibrated, (tables / float(people * recs))[None]


def solution(mesh):
    placed = (
        P(None, ("rec", "tract")),
        P(None, ("rec", "tract")),
        P(("rec", "tract"), None),
        P(("rec", "tract")),
        P(),
        P(),
    )
    return jax.shard_map(
        shards,
        mesh=mesh,
        in_specs=placed,
        out_specs=(P(None, ("rec", "tract")), P("tract", None, "rec")),
        check_vma=False,
    )
```

time: 998 us -> 280 us (0.28)
  other arithmetic: 552 us -> 1.65 us
  matrix products: 118 us -> 0 us
  local copies, waits for them, and re-layouts: 120 us -> 6.23 us
  waiting for transfers between devices: 146 us -> 211 us
  Pallas kernels: 0 us -> 35.6 us
  blocking collectives: 40.1 us -> 7.83 us
    another operation x9 -> x1, other arithmetic: 543 us -> 0.01 us  [shards(): about = jnp.stack([log_income.astype(f32), tract_of[:, 0].astype(f32)])]
    dot_general x19 -> x0, matrix products: 113 us -> none  [the longest x16 81.2 us: gram_step(): jnp.einsum('an,cn->ac', spread, design_block, precision=lax.Precision.HIG...]
    psum x1, waiting for transfers between devices: 74.6 us -> 130 us  [shards(): sums = lax.psum(gram(rep_weights, covariate_codes), ('rec', 'tract'))]
    all_to_all x1 -> x0, waiting for transfers between devices: 47.1 us -> none  [shards(): lax.all_to_all(buffer, 'tract', split_axis=1, concat_axis=1, tiled=True)]
    gather x2 -> x0, local copies, waits for them, and re-layouts: 46.6 us -> none  [shards(): buffer = jnp.take(payload, source.reshape(tract_count, capacity), axis=1)]
    psum x1 -> x0, blocking collectives: 40.1 us -> none  [shards(): gram_sums, totals = lax.psum((gram_sums, totals), ('rec', 'tract'))]
    reduce_scatter x1, waiting for transfers between devices: 23.9 us -> 62 us  [shards(): tables = lax.psum_scatter(tables, 'tract', scatter_dimension=0, tiled=True)]
    pallas_call x0 -> x4, Pallas kernels: none -> 35.6 us  [the longest x1 19.9 us: partial_tables(): pl.pallas_call(functools.partial(table_kernel, tracts), grid=(sources, pe...]
  transfers between devices with their start and end apart: 3 -> 3, of which waited for: 3 -> 3; matrix products, arithmetic and copies ran while one was open for 2% -> 0% of each run, Pallas kernels for 0% -> 0%
where the time goes in v1:
time: 280 us; the launch traced here: 276 us
  waiting for transfers between devices  211 us (75%)
  Pallas kernels  35.6 us (13%)
  between operations  13.8 us (5%)
  blocking collectives  7.83 us (3%)
  local copies, waits for them, and re-layouts  6.23 us (2%)
    psum x1, waiting for transfers between devices, shards(): sums = lax.psum(gram(rep_weights, covariate_codes), ('rec', 'tract'))  130 us
    reduce_scatter x1, waiting for transfers between devices, shards(): tables = lax.psum_scatter(tables, 'tract', scatter_dimension=0, tiled=True)  62 us
    pallas_call x1, Pallas kernels, partial_tables(): pl.pallas_call(functools.partial(table_kernel, tracts), grid=(sources, pe...  19.9 us
    all_gather x1, waiting for transfers between devices, shards(): sent = lax.all_gather(sent, 'rec')  18.1 us
    pallas_call x1, Pallas kernels, gram(): pl.pallas_call(gram_kernel, grid=(people // block,), in_specs=[pl.BlockSp...  7.86 us
    all_gather x1, blocking collectives, shards(): about = lax.all_gather(about, 'rec')  7.83 us
  transfers between devices with their start and end apart: 3, of which 3 were waited for; matrix products, arithmetic and copies ran while one was open for 0% of the time, Pallas kernels for 0%

profile of v1, /device:TPU:11, one launch (start us, length us, event | category | flops | bytes accessed | tf_op | source)
XLA Modules:
  0.0 275.8 jit_solution(1048300493043077333)
XLA Ops:
  7.2 0.0 all-reduce.2.cloned.1.call-start
  7.2 0.0 copy-start.1
  7.2 1.3 copy-done.1
  8.5 0.0 copy-start.4
  8.5 0.9 copy-done.4
  9.4 0.0 copy-start.8
  9.4 7.9 %shard_map.77 = f32[2256,80]{1,0:T(8,128)} custom-call(f32[80,4096]{1,0:T(8,128)S(1)} %copy-done.1, s32[5,4096]{1,0:T(8,128)S(1)} %copy-done.4), custom_call_target="tpu_custom_call" | custom-call | flops 4435476480 | bytes 1310720 | tf_op jit(solution)/shard_map/pallas_call | solution.py:81
  17.3 0.0 all-reduce.2.cloned.1.call-update
  17.3 0.0 all-gather.5.cloned.1.call-start
  17.4 130.4 %all-reduce.2.cloned.1.call-done.sums_ref = f32[2256,80]{1,0:T(8,128)} async-done(((f32[2256,80]{1,0:T(8,128)}), f32[2256,80]{1,0:T(8,128)}) %all-reduce.2.cloned.1.call-update) | async-done | bytes 721936 | tf_op jit(solution)/shard_map/psum | solution.py:267
  147.7 0.0 copy-done.8
  147.7 0.1 broadcast_in_dim.12.controls_ref
  147.8 1.3 copy-done.3
  149.1 5.4 %shard_map.78.x_ref = f32[80,80]{1,0:T(8,128)S(1)} custom-call(f32[2256,80]{1,0:T(8,128)S(1)} %copy-done.3, f32[64,80]{1,0:T(8,128)S(1)} %broadcast_in_dim.12.controls_ref), custom_call_target="tpu_custom_call" | custom-call | tf_op jit(solution)/shard_map/pallas_call | solution.py:159
  154.5 0.0 copy-done.5
  154.5 0.0 copy-done.2
  154.5 0.0 copy-start.7
  154.5 0.0 copy-start.6
  154.6 2.4 shard_map.79
  157.0 0.0 all-gather.5.cloned.1.call-update
  157.0 0.0 reduce-scatter.2.cloned.1.call-start
  157.1 0.0 copy-done.7
  157.1 0.8 dynamic_slice.3
  157.8 0.1 copy.9.grid_ref
  158.0 0.0 copy-done.6
  158.1 7.8 %all-gather.2.about_ref = f32[4,2,4096]{2,1,0:T(2,128)S(1)} all-gather(f32[1,2,4096]{2,1,0:T(2,128)S(1)} %maximum_bitcast_fusion), channel_id=3, replica_groups=mesh['rec'=4,'tract'=8] {'rec'}, dimensions={0}, use_global_device_ids=true | all-gather | bytes 163840 | tf_op jit(solution)/shard_map/all_gather | solution.py:266
  165.9 18.1 %all-gather.5.cloned.1.call-done = bf16[320,4096]{1,0:T(8,128)(2,1)} async-done(((bf16[80,4096]{1,0:T(8,128)(2,1)}), bf16[320,4096]{1,0:T(8,128)(2,1)}) %all-gather.5.cloned.1.call-update) | async-done | bytes 2621456 | tf_op jit(solution)/shard_map/all_gather | solution.py:270
  184.1 1.7 copy-done
  185.8 19.9 %shard_map.80 = f32[640,512]{1,0:T(8,128)} custom-call(bf16[4,80,4096]{2,1,0:T(8,128)(2,1)S(1)} %bitcast.9, f32[4,2,4096]{2,1,0:T(2,128)S(1)} %all-gather.2.about_ref, s32[512,1]{1,0:T(8,128)S(1)} %copy.9.grid_ref), custom_call_target="tpu_custom_call" | custom-call | tf_op jit(solution)/shard_map/pallas_call | solution.py:241
  205.7 0.0 reduce-scatter.2.cloned.1.call-update
  205.7 62.0 %reduce-scatter.2.cloned.1.call-done = f32[80,512]{1,0:T(8,128)} async-done(((f32[640,512]{1,0:T(8,128)}), f32[80,512]{1,0:T(8,128)}) %reduce-scatter.2.cloned.1.call-update) | async-done | bytes 163856 | tf_op jit(solution)/shard_map/reduce_scatter | solution.py:272
  267.7 1.6 multiply_bitcast_fusion
  (7 shorter events, 0.1 us)
Async XLA Ops:
  7.2 140.6 %all-reduce.2.cloned.1.call-start = ((), (), s32[]{:S(2)}) async-start(), calls=%async_computation.1 | async-start | bytes 2310144 | tf_op jit(solution)/shard_map/psum | solution.py:267
  7.2 1.3 copy-start.1
  8.5 0.9 copy-start.4
  9.4 138.3 %copy-start.8 = (f32[64]{0:T(128)S(1)}, f32[64]{0:T(128)}, u32[]{:S(2)}) copy-start(f32[64]{0:T(128)} %param.10) | copy-start | bytes 772
  9.4 145.1 %copy-start.5 = (s32[5,4096]{1,0:T(8,128)S(1)}, s32[5,4096]{1,0:T(8,128)}, u32[]{:S(2)}) copy-start(s32[5,4096]{1,0:T(8,128)} %codes_ref.3) | copy-start | bytes 245764
  17.3 137.2 %copy-start.2 = (f32[80,4096]{1,0:T(8,128)S(1)}, f32[80,4096]{1,0:T(8,128)}, u32[]{:S(2)}) copy-start(f32[80,4096]{1,0:T(8,128)} %w_ref.3) | copy-start | bytes 3932164
  17.3 166.7 %all-gather.5.cloned.1.call-start = ((), (), s32[]{:S(2)}) async-start(), calls=%async_computation.3 | async-start | bytes 3276800 | tf_op jit(solution)/shard_map/all_gather | solution.py:270
  147.8 1.3 copy-start.3
  154.5 2.5 copy-start.7
  154.5 3.5 %copy-start.6 = (s32[4096,1]{0,1:T(1,128)S(1)}, s32[4096,1]{0,1:T(1,128)}, u32[]{:S(2)}) copy-start(s32[4096,1]{0,1:T(1,128)} %param.8) | copy-start | bytes 49156
  157.0 110.7 %reduce-scatter.2.cloned.1.call-start = ((), (), s32[]{:S(2)}) async-start(), calls=%async_computation.2 | async-start | bytes 1474560 | tf_op jit(solution)/shard_map/reduce_scatter | solution.py:272
  184.1 1.7 copy-start
Sparse Core Ops, SparseCore 0:
  17.4 130.2 all-reduce.1
  157.1 26.8 all-gather.4
  205.8 61.8 reduce-scatter.1

commit v2 on v1

--- a/solution.py
+++ b/solution.py
@@ -52,6 +52,7 @@
     @pl.when(step == 0)
     def _():
         total[...] = jnp.zeros_like(total)
+        pairs[rows:, :] = jnp.zeros((pairs.shape[0] - rows, pairs.shape[1]), bf16)
 
     pieces = split3(w_ref[...], 0)
     for (u, v), row in offsets.items():
@@ -73,10 +74,10 @@
         )
 
 
-def gram(rep_weights, covariate_codes):
+def gram(rep_weights, covariate_codes, multiple):
     reps, people = rep_weights.shape
     variables = covariate_codes.shape[0]
-    rows = pair_layout(variables)[2]
+    rows = -(-pair_layout(variables)[2] // multiple) * multiple
     block = 1024
     return pl.pallas_call(
         gram_kernel,
@@ -253,6 +254,149 @@
     )(sent, about, grid_column)
 
 
+def greet(axes):
+    barrier = pltpu.get_barrier_semaphore()
+    count = 0
+    for name, size in axes:
+        me = lax.axis_index(name)
+        for d in range(1, size):
+            pl.semaphore_signal(
+                barrier,
+                inc=1,
+                device_id={name: lax.rem(me + d, size)},
+                device_id_type=pl.DeviceIdType.MESH,
+            )
+            count += 1
+    pl.semaphore_wait(barrier, count)
+
+
+def send(source, target, sems, slot, name, peer):
+    copy = pltpu.make_async_remote_copy(
+        src_ref=source,
+        dst_ref=target,
+        send_sem=sems.at[0, slot],
+        recv_sem=sems.at[1, slot],
+        device_id={name: peer},
+        device_id_type=pl.DeviceIdType.MESH,
+    )
+    copy.start()
+    return copy
+
+
+def total_kernel(
+    recs, tracts, x_ref, about_ref, out_ref, around_ref, from_rec, part, from_tract,
+    about_sems, rec_sems, tract_sems, tract_back, rec_back,
+):
+    rec, tract = lax.axis_index("rec"), lax.axis_index("tract")
+    large, small = part.shape[0], from_tract.shape[1]
+    greet([("rec", recs), ("tract", tracts)])
+
+    arriving = []
+    for d in range(1, recs):
+        peer = lax.rem(rec + d, recs)
+        rows = pl.ds(pl.multiple_of(peer * large, 8), large)
+        arriving.append(send(x_ref.at[rows], from_rec.at[d], rec_sems, d, "rec", peer))
+    about = []
+    for d in range(1, recs):
+        peer = lax.rem(rec + d, recs)
+        about.append(send(about_ref, around_ref.at[rec], about_sems, d, "rec", peer))
+    around_ref[rec] = about_ref[...]
+    for copy in arriving:
+        copy.wait()
+    value = x_ref[pl.ds(pl.multiple_of(rec * large, 8), large), :]
+    for d in range(1, recs):
+        value = value + from_rec[d]
+    part[...] = value
+
+    arriving = []
+    for d in range(1, tracts):
+        peer = lax.rem(tract + d, tracts)
+        rows = pl.ds(pl.multiple_of(peer * small, 8), small)
+        arriving.append(send(part.at[rows], from_tract.at[d], tract_sems, d, "tract", peer))
+    for copy in arriving:
+        copy.wait()
+    value = part[pl.ds(pl.multiple_of(tract * small, 8), small), :]
+    for d in range(1, tracts):
+        value = value + from_tract[d]
+    mine = pl.ds(pl.multiple_of(rec * large + tract * small, 8), small)
+    out_ref[mine, :] = value
+
+    arriving = []
+    for d in range(1, tracts):
+        peer = lax.rem(tract + d, tracts)
+        arriving.append(send(out_ref.at[mine], out_ref.at[mine], tract_back, d, "tract", peer))
+    for copy in arriving:
+        copy.wait()
+    mine = pl.ds(pl.multiple_of(rec * large, 8), large)
+    arriving = []
+    for d in range(1, recs):
+        peer = lax.rem(rec + d, recs)
+        arriving.append(send(out_ref.at[mine], out_ref.at[mine], rec_back, d, "rec", peer))
+    for copy in arriving + about:
+        copy.wait()
+
+
+def totals(x, about, recs, tracts):
+    rows, reps = x.shape
+    large, small = rows // recs, rows // (recs * tracts)
+    dma = pltpu.SemaphoreType.DMA
+    return pl.pallas_call(
+        functools.partial(total_kernel, recs, tracts),
+        in_specs=[pl.BlockSpec(memory_space=pltpu.VMEM)] * 2,
+        out_specs=[pl.BlockSpec(memory_space=pltpu.VMEM)] * 2,
+        out_shape=[
+            jax.ShapeDtypeStruct((rows, reps), f32),
+            jax.ShapeDtypeStruct((recs,) + about.shape, f32),
+        ],
+        scratch_shapes=[
+            pltpu.VMEM((recs, large, reps), f32),
+            pltpu.VMEM((large, reps), f32),
+            pltpu.VMEM((tracts, small, reps), f32),
+            dma((2, recs)),
+            dma((2, recs)),
+            dma((2, tracts)),
+            dma((2, tracts)),
+            dma((2, recs)),
+        ],
+        compiler_params=pltpu.CompilerParams(
+            vmem_limit_bytes=vmem_bytes, collective_id=0, has_side_effects=True
+        ),
+    )(x, about)
+
+
+def scatter_kernel(tracts, scale, x_ref, out_ref, landed, sems):
+    tract = lax.axis_index("tract")
+    reps = out_ref.shape[1]
+    greet([("tract", tracts)])
+    arriving = []
+    for d in range(1, tracts):
+        peer = lax.rem(tract + d, tracts)
+        rows = pl.ds(pl.multiple_of(peer * reps, 8), reps)
+        arriving.append(send(x_ref.at[rows], landed.at[d], sems, d, "tract", peer))
+    value = x_ref[pl.ds(pl.multiple_of(tract * reps, 8), reps), :]
+    for d in range(1, tracts):
+        arriving[d - 1].wait()
+        value = value + landed[d]
+    out_ref[0] = value / scale
+
+
+def scatter(x, reps, tracts, scale):
+    columns = x.shape[1]
+    return pl.pallas_call(
+        functools.partial(scatter_kernel, tracts, scale),
+        in_specs=[pl.BlockSpec(memory_space=pltpu.VMEM)],
+        out_specs=pl.BlockSpec(memory_space=pltpu.VMEM),
+        out_shape=jax.ShapeDtypeStruct((1, reps, columns), f32),
+        scratch_shapes=[
+            pltpu.VMEM((tracts, reps, columns), f32),
+            pltpu.SemaphoreType.DMA((2, tracts)),
+        ],
+        compiler_params=pltpu.CompilerParams(
+            vmem_limit_bytes=vmem_bytes, collective_id=1, has_side_effects=True
+        ),
+    )(x)
+
+
 def shards(rep_weights, covariate_codes, tract_of, log_income, controls, threshold_grid):
     reps, people = rep_weights.shape
     variables = covariate_codes.shape[0]
@@ -263,14 +407,13 @@
         threshold_grid, lax.axis_index("rec") * share, share, 0
     )[:, None]
     about = jnp.stack([log_income.astype(f32), tract_of[:, 0].astype(f32)])
-    about = lax.all_gather(about, "rec")
-    sums = lax.psum(gram(rep_weights, covariate_codes), ("rec", "tract"))
+    sums = gram(rep_weights, covariate_codes, 8 * recs * tracts)
+    sums, about = totals(sums, about, recs, tracts)
     x = solve(sums, controls, variables)
     calibrated, sent = calibrate(x, rep_weights, covariate_codes)
     sent = lax.all_gather(sent, "rec")
     tables = partial_tables(sent, about, grid_column, tracts)
-    tables = lax.psum_scatter(tables, "tract", scatter_dimension=0, tiled=True)
-    return calibrated, (tables / float(people * recs))[None]
+    return calibrated, scatter(tables, reps, tracts, float(people * recs))
 
 
 def solution(mesh):

time: 280 us -> 163 us (0.58); the launches traced: 276 us -> 163 us
  waiting for transfers between devices: 211 us -> 25.8 us
  Pallas kernels: 35.6 us -> 116 us
  blocking collectives: 7.83 us -> 0 us
    psum x1 -> x0, waiting for transfers between devices: 130 us -> none  [shards(): sums = lax.psum(gram(rep_weights, covariate_codes), ('rec', 'tract'))]
    pallas_call x0 -> x2, Pallas kernels: none -> 80.5 us  [the longest x1 47.7 us: totals(): pl.pallas_call(functools.partial(total_kernel, recs, tracts), in_specs=[p...]
    reduce_scatter x1 -> x0, waiting for transfers between devices: 62 us -> none  [shards(): tables = lax.psum_scatter(tables, 'tract', scatter_dimension=0, tiled=True)]
    all_gather x1 -> x0, blocking collectives: 7.83 us -> none  [shards(): about = lax.all_gather(about, 'rec')]
    all_gather x1, waiting for transfers between devices: 18.1 us -> 25.7 us  [shards(): sent = lax.all_gather(sent, 'rec')]
  transfers between devices with their start and end apart: 3 -> 1, of which waited for: 3 -> 1; matrix products, arithmetic and copies ran while one was open for 0% -> 1% of each run, Pallas kernels for 0% -> 0%
where the time goes in v2:
time: 163 us
  Pallas kernels  116 us (71%)
  waiting for transfers between devices  25.8 us (16%)
  between operations  14.1 us (9%)
  local copies, waits for them, and re-layouts  5.62 us (3%)
    pallas_call x1, Pallas kernels, totals(): pl.pallas_call(functools.partial(total_kernel, recs, tracts), in_specs=[p...  47.7 us
    pallas_call x1, Pallas kernels, scatter(): pl.pallas_call(functools.partial(scatter_kernel, tracts, scale), in_specs...  32.8 us
    all_gather x1, waiting for transfers between devices, shards(): sent = lax.all_gather(sent, 'rec')  25.7 us
    pallas_call x1, Pallas kernels, partial_tables(): pl.pallas_call(functools.partial(table_kernel, tracts), grid=(sources, pe...  18.8 us
    pallas_call x1, Pallas kernels, gram(): pl.pallas_call(gram_kernel, grid=(people // block,), in_specs=[pl.BlockSp...  8.47 us
    pallas_call x1, Pallas kernels, solve(): pl.pallas_call(functools.partial(solve_kernel, variables), in_specs=[pl.B...  5.44 us
    unnamed x11, local copies, waits for them, and re-layouts  4.63 us
  transfers between devices with their start and end apart: 1, of which 1 were waited for; matrix products, arithmetic and copies ran while one was open for 1% of the time, Pallas kernels for 0%

profile of v2, /device:TPU:11, one launch (start us, length us, event | category | flops | bytes accessed | tf_op | source)
XLA Modules:
  0.0 162.6 jit_solution(5301677454327253195)
XLA Ops:
  7.2 0.0 all-gather.3.cloned.1.call-start
  7.2 0.7 convert_bitcast_fusion
  7.9 0.7 stack.13
  8.7 0.0 copy-start.1
  8.7 1.3 copy-done.1
  10.0 0.0 copy-start.3
  10.0 0.9 copy-done.3
  10.9 0.0 copy-start.4
  10.9 8.5 %shard_map.77.x_ref = f32[2304,80]{1,0:T(8,128)S(1)} custom-call(f32[80,4096]{1,0:T(8,128)S(1)} %copy-done.1, s32[5,4096]{1,0:T(8,128)S(1)} %copy-done.3), custom_call_target="tpu_custom_call" | custom-call | flops 4529848320 | bytes 1310720 | tf_op jit(solution)/shard_map/pallas_call | solution.py:82
  19.4 0.0 copy-start.2
  19.4 47.7 %shard_map.78 = (f32[2304,80]{1,0:T(8,128)S(1)}, f32[4,2,4096]{2,1,0:T(2,128)S(1)}) custom-call(f32[2304,80]{1,0:T(8,128)S(1)} %shard_map.77.x_ref, f32[2,4096]{1,0:T(2,128)S(1)} %pad_maximum_fusion.about_ref), custom_call_target="tpu_custom_call" | custom-call | tf_op jit(solution)/shard_map/pallas_call | solution.py:343
  67.1 0.0 copy-done.4
  67.1 0.1 broadcast_in_dim.4.controls_ref
  67.2 5.4 %shard_map.79.x_ref = f32[80,80]{1,0:T(8,128)S(1)} custom-call(f32[2304,80]{1,0:T(8,128)S(1)} %get-tuple-element.6.sums_ref, f32[64,80]{1,0:T(8,128)S(1)} %broadcast_in_dim.4.controls_ref), custom_call_target="tpu_custom_call" | custom-call | tf_op jit(solution)/shard_map/pallas_call | solution.py:160
  72.6 0.0 copy-done.2
  72.6 2.4 %shard_map.80 = (f32[80,4096]{1,0:T(8,128)}, bf16[80,4096]{1,0:T(8,128)(2,1)}) custom-call(f32[80,80]{1,0:T(8,128)S(1)} %shard_map.79.x_ref, f32[80,4096]{1,0:T(8,128)S(1)} %copy-done.2, s32[5,4096]{1,0:T(8,128)S(1)} %copy-done.3), custom_call_target="tpu_custom_call" | custom-call | tf_op jit(solution)/shard_map/pallas_call | solution.py:196
  75.1 0.0 all-gather.3.cloned.1.call-update
  75.1 0.8 dynamic_slice.3
  75.9 0.1 copy.8.grid_ref
  76.0 25.7 %all-gather.3.cloned.1.call-done = bf16[320,4096]{1,0:T(8,128)(2,1)} async-done(((bf16[80,4096]{1,0:T(8,128)(2,1)}), bf16[320,4096]{1,0:T(8,128)(2,1)}) %all-gather.3.cloned.1.call-update) | async-done | bytes 2621456 | tf_op jit(solution)/shard_map/all_gather | solution.py:414
  101.8 0.0 copy-start
  101.8 1.7 %copy-done = bf16[320,4096]{1,0:T(8,128)(2,1)S(1)} copy-done((bf16[320,4096]{1,0:T(8,128)(2,1)S(1)}, bf16[320,4096]{1,0:T(8,128)(2,1)}, u32[]{:S(2)}) %copy-start) | copy-done | bytes 2621464
  103.5 18.8 %shard_map.81.x_ref = f32[640,512]{1,0:T(8,128)S(1)} custom-call(bf16[4,80,4096]{2,1,0:T(8,128)(2,1)S(1)} %bitcast.5, f32[4,2,4096]{2,1,0:T(2,128)S(1)} %get-tuple-element.9.about_ref, s32[512,1]{1,0:T(8,128)S(1)} %copy.8.grid_ref), custom_call_target="tpu_custom_call" | custom-call | tf_op jit(solution)/shard_map/pallas_call | solution.py:242
  122.3 32.8 %shard_map.82 = f32[1,80,512]{2,1,0:T(8,128)S(1)} custom-call(f32[640,512]{1,0:T(8,128)S(1)} %shard_map.81.x_ref), custom_call_target="tpu_custom_call" | custom-call | tf_op jit(solution)/shard_map/pallas_call | solution.py:385
  155.1 0.7 copy.10
  (1 shorter events, 0.0 us)
Async XLA Ops:
  7.2 94.6 %all-gather.3.cloned.1.call-start = ((), (), s32[]{:S(2)}) async-start(), calls=%async_computation | async-start | bytes 3276800 | tf_op jit(solution)/shard_map/all_gather | solution.py:414
  8.7 1.3 copy-start.1
  10.0 0.9 copy-start.3
  10.9 56.2 %copy-start.4 = (f32[64]{0:T(128)S(1)}, f32[64]{0:T(128)}, u32[]{:S(2)}) copy-start(f32[64]{0:T(128)} %param.10) | copy-start | bytes 772
  19.4 53.2 %copy-start.2 = (f32[80,4096]{1,0:T(8,128)S(1)}, f32[80,4096]{1,0:T(8,128)}, u32[]{:S(2)}) copy-start(f32[80,4096]{1,0:T(8,128)} %w_ref.3) | copy-start | bytes 3932164
  101.8 1.7 %copy-start = (bf16[320,4096]{1,0:T(8,128)(2,1)S(1)}, bf16[320,4096]{1,0:T(8,128)(2,1)}, u32[]{:S(2)}) copy-start(bf16[320,4096]{1,0:T(8,128)(2,1)} %all-gather.3.cloned.1.call-done) | copy-start | bytes 7864324
Sparse Core Ops, SparseCore 0:
  75.2 26.5 all-gather.2
